TPU v7x, 32 devices: a whole 2x2x4 slice. The times are simulated.
32 devices in a mesh: dp: 16 (over z, y, x), tensor: 2 (over core).
Axes of the slice: x: 2, y: 2, z: 4, core: 2. Of those that a mesh axis runs over, the one named last changes fastest.
Arguments:
- tokens: bfloat16 [25216, 768], P(('dp', 'tensor')), may hold values from -6 to 6
- cotangent: bfloat16 [25216, 768], P(('dp', 'tensor')), may hold values from -6 to 6
- norm1_gain: bfloat16 [768], P(('dp', 'tensor')), may hold values from 0.25 to 1.75
- norm1_shift: bfloat16 [768], P(('dp', 'tensor')), may hold values from -3 to 3
- qkv_weight: bfloat16 [3, 768, 768], P(None, 'dp', 'tensor'), may hold values from -16 to 16
- qv_bias: bfloat16 [2, 2, 384], P(None, 'tensor', 'dp'), may hold values from -3 to 3
- out_weight: bfloat16 [768, 768], P('tensor', 'dp'), may hold values from -1.75 to 1.75
- out_bias: bfloat16 [768], P(('dp', 'tensor')), may hold values from -3 to 3
- norm2_gain: bfloat16 [768], P(('dp', 'tensor')), may hold values from 0.25 to 1.75
- norm2_shift: bfloat16 [768], P(('dp', 'tensor')), may hold values from -3 to 3
- up_weight: bfloat16 [768, 3072], P('dp', 'tensor'), may hold values from -0.21875 to 0.21875
- up_bias: bfloat16 [2, 1536], P('tensor', 'dp'), may hold values from -3 to 3
- down_weight: bfloat16 [3072, 768], P('tensor', 'dp'), may hold values from -0.15625 to 0.15625
- down_bias: bfloat16 [768], P(('dp', 'tensor')), may hold values from -3 to 3
Outputs:
- layer_out: bfloat16 [25216, 768], P(('dp', 'tensor'))
- input_grad: float32 [25216, 768], P(('dp', 'tensor'))
- grad_norm1_gain: float32 [768], P(('dp', 'tensor'))
- grad_norm1_shift: float32 [768], P(('dp', 'tensor'))
- grad_qkv_weight: float32 [3, 768, 768], P(None, 'dp', 'tensor')
- grad_qv_bias: float32 [2, 2, 384], P(None, 'tensor', 'dp')
- grad_out_weight: float32 [768, 768], P('tensor', 'dp')
- grad_out_bias: float32 [768], P(('dp', 'tensor'))
- grad_norm2_gain: float32 [768], P(('dp', 'tensor'))
- grad_norm2_shift: float32 [768], P(('dp', 'tensor'))
- grad_up_weight: float32 [768, 3072], P('dp', 'tensor')
- grad_up_bias: float32 [2, 1536], P('tensor', 'dp')
- grad_down_weight: float32 [3072, 768], P('tensor', 'dp')
- grad_down_bias: float32 [768], P(('dp', 'tensor'))
All inputs are finite; a program needn't handle non-finite values.
Results may differ from a plain program's by a relative error of at most 0.018.
Values may be sent and summed in bfloat16 or wider, within the bound.
A program may use at most 128 MiB of HBM per device.

v0:
```python
from functools import partial

import jax
import jax.numpy as jnp
from jax import lax
from jax.sharding import PartitionSpec as P

HD = 64
SEQ = 197


epsilon = 1e-06


def normalize(values):
    centered = values - jnp.mean(values, axis=-1, keepdims=True)
    inverse = lax.rsqrt(jnp.mean(centered * centered, axis=-1, keepdims=True) + epsilon)
    return (centered * inverse, inverse)


def norm_back(grad_out, normed, inverse, gain):
    d_normed = grad_out * gain
    grad_in = inverse * (
        d_normed
        - jnp.mean(d_normed, axis=-1, keepdims=True)
        - normed * jnp.mean(d_normed * normed, axis=-1, keepdims=True)
    )
    return (grad_in, jnp.sum(grad_out * normed, axis=0), jnp.sum(grad_out, axis=0))


def gather_rows(rows):
    return lax.all_gather(rows, "tensor", axis=0, tiled=True)


def sum_rows(terms):
    return lax.psum_scatter(
        terms.astype(jnp.bfloat16), "tensor", scatter_dimension=0, tiled=True
    ).astype(jnp.float32)


def gather_grads(rows):
    return lax.all_gather(rows, "tensor", axis=0, tiled=True)


def sum_grads(terms):
    return lax.psum_scatter(
        terms.astype(jnp.bfloat16), "tensor", scatter_dimension=0, tiled=True
    ).astype(jnp.float32)


def split_heads(matrix):
    return matrix.reshape(matrix.shape[0] // SEQ, SEQ, matrix.shape[1] // HD, HD)


def attend(queries, keys, values):
    scores = jnp.einsum(
        "iqhd,ikhd->ihqk", queries, keys, preferred_element_type=jnp.float32
    ) * HD ** (-0.5)
    row_top = jnp.max(scores, axis=-1, keepdims=True)
    shifted = jnp.exp(scores - row_top)
    row_total = jnp.sum(shifted, axis=-1, keepdims=True)
    probs = (shifted / row_total).astype(jnp.bfloat16)
    attended = jnp.einsum("ihqk,ikhd->iqhd", probs, values, preferred_element_type=jnp.float32)
    return (attended.astype(jnp.bfloat16), row_top + jnp.log(row_total))


def attend_back(queries, keys, values, log_total, d_attended):
    factor = HD ** (-0.5)
    scores = (
        jnp.einsum("iqhd,ikhd->ihqk", queries, keys, preferred_element_type=jnp.float32) * factor
    )
    probs = jnp.exp(scores - log_total)
    probs_low = probs.astype(jnp.bfloat16)
    grad_values = jnp.einsum(
        "ihqk,iqhd->ikhd", probs_low, d_attended, preferred_element_type=jnp.float32
    ).astype(jnp.bfloat16)
    d_probs = jnp.einsum("iqhd,ikhd->ihqk", d_attended, values, preferred_element_type=jnp.float32)
    d_scores = (probs * (d_probs - jnp.sum(probs * d_probs, axis=-1, keepdims=True))).astype(
        jnp.bfloat16
    )
    grad_queries = (
        jnp.einsum("ihqk,ikhd->iqhd", d_scores, keys, preferred_element_type=jnp.float32) * factor
    ).astype(jnp.bfloat16)
    grad_keys = (
        jnp.einsum("ihqk,iqhd->ikhd", d_scores, queries, preferred_element_type=jnp.float32)
        * factor
    ).astype(jnp.bfloat16)
    return (grad_queries, grad_keys, grad_values)


def local(
    tokens,
    cotangent,
    norm1_gain,
    norm1_shift,
    qkv_weight,
    qv_bias,
    out_weight,
    out_bias,
    norm2_gain,
    norm2_shift,
    up_weight,
    up_bias,
    down_weight,
    down_bias,
):
    small_full = (
        lax.all_gather(norm1_gain, ("dp", "tensor"), axis=0, tiled=True),
        lax.all_gather(norm1_shift, ("dp", "tensor"), axis=0, tiled=True),
        lax.all_gather(out_bias, ("dp", "tensor"), axis=0, tiled=True),
        lax.all_gather(norm2_gain, ("dp", "tensor"), axis=0, tiled=True),
        lax.all_gather(norm2_shift, ("dp", "tensor"), axis=0, tiled=True),
        lax.all_gather(down_bias, ("dp", "tensor"), axis=0, tiled=True),
    )
    gain_one, shift_one, out_vec, gain_two, shift_two, down_vec = [
        item.astype(jnp.float32) for item in small_full
    ]
    qkv_full, qv_full, out_full = (
        lax.all_gather(qkv_weight, "dp", axis=1, tiled=True),
        lax.all_gather(qv_bias, "dp", axis=2, tiled=True),
        lax.all_gather(out_weight, "dp", axis=1, tiled=True),
    )
    inputs = tokens.astype(jnp.float32)
    normed_one, inverse_one = normalize(inputs)
    h_one = gather_rows((normed_one * gain_one + shift_one).astype(jnp.bfloat16))
    projected = jnp.einsum("gd,tde->tge", h_one, qkv_full, preferred_element_type=jnp.float32)
    qv_rows = qv_full.astype(jnp.float32)
    queries = split_heads((projected[0] + qv_rows[0, 0]).astype(jnp.bfloat16))
    keys = split_heads(projected[1].astype(jnp.bfloat16))
    values = split_heads((projected[2] + qv_rows[1, 0]).astype(jnp.bfloat16))
    attended_heads, log_total = attend(queries, keys, values)
    group_rows = h_one.shape[0]
    attended = attended_heads.reshape(group_rows, qkv_full.shape[2])
    branch_one = sum_rows(jnp.dot(attended, out_full, preferred_element_type=jnp.float32)) + out_vec
    middle = inputs + branch_one
    up_full, up_vec, down_full = (
        lax.all_gather(up_weight, "dp", axis=0, tiled=True),
        lax.all_gather(up_bias, "dp", axis=1, tiled=True),
        lax.all_gather(down_weight, "dp", axis=1, tiled=True),
    )
    normed_two, inverse_two = normalize(middle)
    h_two = gather_rows((normed_two * gain_two + shift_two).astype(jnp.bfloat16))
    pre_act = jnp.dot(h_two, up_full, preferred_element_type=jnp.float32) + up_vec[0].astype(
        jnp.float32
    )
    hidden = jax.nn.gelu(pre_act, approximate=False).astype(jnp.bfloat16)
    branch_two = sum_rows(jnp.dot(hidden, down_full, preferred_element_type=jnp.float32)) + down_vec
    layer_out = (middle + branch_two).astype(jnp.bfloat16)
    grad_rows = cotangent.astype(jnp.float32)
    grad_down_bias = jnp.sum(grad_rows, axis=0)
    cot_all = gather_grads(cotangent)
    grad_down = jnp.einsum("gf,gd->fd", hidden, cot_all, preferred_element_type=jnp.float32)
    d_hidden = jnp.einsum("gd,fd->gf", cot_all, down_full, preferred_element_type=jnp.float32)
    gelu_out, gelu_back = jax.vjp(partial(jax.nn.gelu, approximate=False), pre_act)
    d_pre = gelu_back(d_hidden)[0].astype(jnp.bfloat16)
    grad_up_bias = jnp.sum(d_pre.astype(jnp.float32), axis=0)[None, :]
    grad_up = jnp.einsum("gd,gf->df", h_two, d_pre, preferred_element_type=jnp.float32)
    d_h_two = sum_grads(jnp.einsum("gf,df->gd", d_pre, up_full, preferred_element_type=jnp.float32))
    d_middle, grad_gain_two, grad_shift_two = norm_back(d_h_two, normed_two, inverse_two, gain_two)
    d_middle = d_middle + grad_rows
    d_branch = d_middle.astype(jnp.bfloat16)
    grad_out_bias = jnp.sum(d_branch.astype(jnp.float32), axis=0)
    branch_all = gather_grads(d_branch)
    grad_out = jnp.einsum("ge,gd->ed", attended, branch_all, preferred_element_type=jnp.float32)
    d_attended = jnp.einsum(
        "gd,ed->ge", branch_all, out_full, preferred_element_type=jnp.float32
    ).astype(jnp.bfloat16)
    grad_queries, grad_keys, grad_values = attend_back(
        queries, keys, values, log_total, split_heads(d_attended)
    )
    width = qkv_full.shape[2]
    grad_stack = jnp.stack(
        [
            grad_queries.reshape(group_rows, width),
            grad_keys.reshape(group_rows, width),
            grad_values.reshape(group_rows, width),
        ]
    )
    grad_qv = jnp.stack(
        [
            jnp.sum(grad_stack[0].astype(jnp.float32), axis=0),
            jnp.sum(grad_stack[2].astype(jnp.float32), axis=0),
        ]
    )[:, None, :]
    grad_qkv = jnp.einsum("gd,tge->tde", h_one, grad_stack, preferred_element_type=jnp.float32)
    d_h_one = sum_grads(
        jnp.einsum("tge,tde->gd", grad_stack, qkv_full, preferred_element_type=jnp.float32)
    )
    share_qkv, share_qv, share_out, share_up, share_up_bias, share_down = (
        lax.psum_scatter(grad_qkv, "dp", scatter_dimension=1, tiled=True),
        lax.psum_scatter(grad_qv, "dp", scatter_dimension=2, tiled=True),
        lax.psum_scatter(grad_out, "dp", scatter_dimension=1, tiled=True),
        lax.psum_scatter(grad_up, "dp", scatter_dimension=0, tiled=True),
        lax.psum_scatter(grad_up_bias, "dp", scatter_dimension=1, tiled=True),
        lax.psum_scatter(grad_down, "dp", scatter_dimension=1, tiled=True),
    )
    d_input, grad_gain_one, grad_shift_one = norm_back(d_h_one, normed_one, inverse_one, gain_one)
    input_grad = d_middle + d_input
    small_shares = (
        lax.psum_scatter(grad_gain_one, ("dp", "tensor"), scatter_dimension=0, tiled=True),
        lax.psum_scatter(grad_shift_one, ("dp", "tensor"), scatter_dimension=0, tiled=True),
        lax.psum_scatter(grad_out_bias, ("dp", "tensor"), scatter_dimension=0, tiled=True),
        lax.psum_scatter(grad_gain_two, ("dp", "tensor"), scatter_dimension=0, tiled=True),
        lax.psum_scatter(grad_shift_two, ("dp", "tensor"), scatter_dimension=0, tiled=True),
        lax.psum_scatter(grad_down_bias, ("dp", "tensor"), scatter_dimension=0, tiled=True),
    )
    return (
        layer_out,
        input_grad,
        small_shares[0],
        small_shares[1],
        share_qkv,
        share_qv,
        share_out,
        small_shares[2],
        small_shares[3],
        small_shares[4],
        share_up,
        share_up_bias,
        share_down,
        small_shares[5],
    )


def solution(mesh):
    placed = (
        P(("dp", "tensor"), None),
        P(("dp", "tensor"), None),
        P(("dp", "tensor")),
        P(("dp", "tensor")),
        P(None, "dp", "tensor"),
        P(None, "tensor", "dp"),
        P("tensor", "dp"),
        P(("dp", "tensor")),
        P(("dp", "tensor")),
        P(("dp", "tensor")),
        P("dp", "tensor"),
        P("tensor", "dp"),
        P("tensor", "dp"),
        P(("dp", "tensor")),
    )
    return jax.shard_map(
        local,
        mesh=mesh,
        in_specs=placed,
        out_specs=(
            P(("dp", "tensor"), None),
            P(("dp", "tensor"), None),
            P(("dp", "tensor")),
            P(("dp", "tensor")),
            P(None, "dp", "tensor"),
            P(None, "tensor", "dp"),
            P("tensor", "dp"),
            P(("dp", "tensor")),
            P(("dp", "tensor")),
            P(("dp", "tensor")),
            P("dp", "tensor"),
            P("tensor", "dp"),
            P("tensor", "dp"),
            P(("dp", "tensor")),
        ),
        check_vma=False,
    )
```

profile of v0, /device:TPU:0, one launch (start us, length us, event | category | flops | bytes accessed | tf_op | source)
XLA Modules:
  0.0 1153.3 jit_solution(2900009696811488194)
XLA Ops:
  12.4 42.2 %all-reduce.24 = (bf16[768]{0:T(1024)(128)(2,1)S(1)}, bf16[768]{0:T(1024)(128)(2,1)S(1)}, bf16[768]{0:T(1024)(128)(2,1)S(1)}, bf16[768]{0:T(1024)(128)(2,1)S(1)}...) all-reduce(bf16[768]{0:T(1024)(128)(2,1)S(1)} %dynamic-update-slice, ...), channel_id=1, replica_groups=mesh['dp'=16,'tensor'=2] {'dp','tensor'}, use_global_device_ids=true, to_apply=%add.4 | all-reduce | flops 4608 | bytes 18432
  61.2 41.0 %all_gather.52 = bf16[2,1,384]{1,0,2:T(2,128)(2,1)S(1)} all-gather(bf16[2,1,24]{1,0,2:T(2,128)(2,1)S(1)} %copy.90), channel_id=1, replica_groups=mesh['dp'=16,'tensor'=2] {'dp'}, dimensions={2}, use_global_device_ids=true | all-gather | bytes 1632 | tf_op jit(solution)/shard_map/all_gather | solution.py:120
  104.1 40.2 %all_gather.53 = bf16[384,768]{0,1:T(8,128)(2,1)S(1)} all-gather(bf16[384,48]{0,1:T(8,128)(2,1)S(1)} %copy-done.24), channel_id=1, replica_groups=mesh['dp'=16,'tensor'=2] {'dp'}, dimensions={1}, use_global_device_ids=true | all-gather | bytes 626688 | tf_op jit(solution)/shard_map/all_gather | solution.py:121
  144.2 3.8 reshape.144
  148.1 5.5 convolution_bitcast_fusion
  153.7 2.6 fusion.62
  156.3 3.6 copy.89
  159.9 5.1 squeeze.8
  165.0 3.4 reshape.160
  168.4 4.6 copy.94
  173.0 3.3 copy.91
  176.3 5.1 squeeze.9
  181.4 2.5 add_convert_fusion.2
  191.8 2.5 fusion.46
  196.3 4.5 reshape.114
  200.8 4.2 convolution_convert_fusion.2
  205.0 6.4 fusion
  211.4 2.3 collective-permute-start
  215.0 5.0 concatenate
  226.5 38.4 %all-reduce.5 = bf16[1536]{0:T(1024)(128)(2,1)S(1)} all-reduce(bf16[1536]{0:T(1024)(128)(2,1)S(1)} %dynamic-update-slice.5), channel_id=1, replica_groups=mesh['dp'=16,'tensor'=2] {'dp'}, use_global_device_ids=true, to_apply=%add.5 | all-reduce | flops 1536 | bytes 6144
  264.9 3.6 reshape.137
  268.5 3.5 reshape.135
  272.1 26.6 %all-gather.14.cloned.1.call-done = bf16[768,1536]{1,0:T(8,128)(2,1)} async-done(((bf16[48,1536]{1,0:T(8,128)(2,1)}), bf16[768,1536]{1,0:T(8,128)(2,1)}) %all-gather.14.cloned.1.call-update) | async-done | bytes 2359312 | tf_op jit(solution)/shard_map/all_gather | solution.py:137
  298.7 27.7 %multiply_convert_fusion.1 = (bf16[1576,1536]{1,0:T(8,128)(2,1)}, f32[1576,1536]{1,0:T(8,128)}, f32[1576,1536]{1,0:T(8,128)}) fusion(f32[1536]{0:T(1024)S(1)} %add.175, bf16[1576,768]{1,0:T(8,128)(2,1)} %reshape.135, bf16[768,1536]{1,0:T(8,128)(2,1)} %all-gather.14.cloned.1.call-done), kind=kOutput, calls=%fused_computation.9 | convolution fusion | flops 3878019072 | bytes 28993536 | tf_op jit(solution)/shard_map/dot_general | solution.py:143
  326.4 36.1 %all-gather.16.cloned.1.call-done = bf16[1536,768]{0,1:T(8,128)(2,1)} async-done(((bf16[1536,48]{0,1:T(8,128)(2,1)}), bf16[1536,768]{0,1:T(8,128)(2,1)}) %all-gather.16.cloned.1.call-update) | async-done | bytes 2359312 | tf_op jit(solution)/shard_map/all_gather | solution.py:139
  362.5 13.3 %convert_reduce_fusion = (f32[1536]{0:T(1024)S(1)}, bf16[1576,1536]{1,0:T(8,128)(2,1)S(1)}) fusion(f32[1576,1536]{1,0:T(8,128)} %get-tuple-element.99, f32[1576,1536]{1,0:T(8,128)} %get-tuple-element.109, bf16[1576,768]{1,0:T(8,128)(2,1)} %reshape.137, bf16[1536,768]{0,1:T(8,128)(2,1)} %all-gather.16.cloned.1.call-done), kind=kOutput, calls=%fused_computation.7 | convolution fusion | flops 3756980736 | bytes 28993536 | tf_op jit(solution)/shard_map/gd,fd->gf/dot_general | solution.py:153
  378.0 5.2 convolution_convert_fusion
  383.3 7.0 fusion.2
  391.0 2.3 collective-permute-start.2
  394.1 7.1 concatenate.2
  401.2 3.4 fusion.37
  410.8 8.8 all-gather.24.cloned.1.call-done
  419.5 3.6 reshape.139
  423.1 4.1 convolution_convert_fusion.3
  427.2 5.0 reshape.161
  432.2 4.6 copy.99
  436.8 7.7 convert_reduce_fusion.4
  444.6 7.6 multiply_reduce_fusion
  452.2 12.2 %multiply_convert_fusion = bf16[8,6,197,197]{2,3,1,0:T(8,128)(2,1)} fusion(f32[8,6,197,197]{2,3,1,0:T(8,128)} %get-tuple-element.111, f32[8,6,197,197]{2,3,1,0:T(8,128)} %copy-done, f32[8,6,197]{2,1,0:T(8,128)S(1)} %get-tuple-element.110, f32[8,6,197]{2,1,0:T(8,128)S(1)} %log_add_fusion), kind=kLoop, calls=%fused_computation.1 | loop fusion | flops 9314160 | bytes 18703968 | tf_op jit(solution)/shard_map/convert_element_type | solution.py:78
  464.4 5.9 fusion.48
  472.6 4.7 copy.121
  477.2 5.2 reshape.149
  482.4 4.7 copy.120
  487.1 5.2 reshape.148
  492.3 4.7 copy.119
  497.0 5.6 reshape.147
  506.7 5.5 convolution_bitcast_fusion.1
  512.2 6.2 copy.113
  518.5 4.7 fusion.64
  523.3 9.9 fusion.65
  533.4 9.8 fusion.66
  544.6 8.6 convolution_convert_fusion.1
  554.7 7.4 bitcast_convert_fusion
  562.1 9.9 fusion.60
  576.8 43.6 %all-reduce.14 = f32[2,1,384]{2,1,0:T(1,128)S(1)} all-reduce(f32[2,1,384]{2,1,0:T(1,128)S(1)} %broadcast_in_dim.4), channel_id=9, replica_groups=mesh['dp'=16,'tensor'=2] {'dp'}, use_global_device_ids=true, to_apply=%region_22.0.clone | all-reduce | flops 768 | bytes 6144
  621.1 7.2 concatenate.3
  628.3 2.7 fusion.38
  631.0 37.7 %all-reduce.23 = (f32[768]{0:T(1024)S(1)}, f32[768]{0:T(1024)S(1)}, f32[768]{0:T(1024)S(1)}, f32[768]{0:T(1024)S(1)}, f32[768]{0:T(1024)S(1)}, /*index=5*/f32[768]{0:T(1024)S(1)}) all-reduce(f32[768]{0:T(1024)S(1)} %get-tuple-element.72, f32[768]{0:T(1024)S(1)} %get-tuple-element.77, ...), channel_id=6, replica_groups=mesh['dp'=16,'tensor'=2] {'dp','tensor'}, use_global_device_ids=true, to_apply=%region_16.0.clone | all-reduce | flops 4608 | bytes 36864
  672.2 7.2 concatenate.1
  679.4 5.3 fusion.31
  684.7 48.4 %all-reduce.28.cloned.1.call-done = f32[3,768,384]{2,0,1:T(4,128)} async-done(((f32[3,768,384]{2,0,1:T(4,128)}), f32[3,768,384]{2,0,1:T(4,128)}) %all-reduce.28.cloned.1.call-update) | async-done | bytes 3538960
  734.8 126.8 %reduce-scatter.16.cloned.1.call-done = f32[384,48]{0,1:T(8,128)} async-done(((f32[384,768]{0,1:T(8,128)}), f32[384,48]{0,1:T(8,128)}) %reduce-scatter.16.cloned.1.call-update) | async-done | bytes 73744 | tf_op jit(solution)/shard_map/reduce_scatter | solution.py:192
  861.6 142.8 %reduce-scatter.18.cloned.1.call-done = f32[48,1536]{1,0:T(8,128)} async-done(((f32[768,1536]{1,0:T(8,128)}), f32[48,1536]{1,0:T(8,128)}) %reduce-scatter.18.cloned.1.call-update) | async-done | bytes 294928 | tf_op jit(solution)/shard_map/reduce_scatter | solution.py:193
  1004.4 141.9 %reduce-scatter.20.cloned.1.call-done = f32[1536,48]{0,1:T(8,128)} async-done(((f32[1536,768]{0,1:T(8,128)}), f32[1536,48]{0,1:T(8,128)}) %reduce-scatter.20.cloned.1.call-update) | async-done | bytes 294928 | tf_op jit(solution)/shard_map/reduce_scatter | solution.py:195
  (171 shorter events, 58.7 us)
Async XLA Ops:
  7.2 50.7 %copy-start.1 = (bf16[788,768]{1,0:T(8,128)(2,1)S(1)}, bf16[788,768]{1,0:T(8,128)(2,1)}, u32[]{:S(2)}) copy-start(bf16[788,768]{1,0:T(8,128)(2,1)} %param.14) | copy-start | bytes 3631108
  7.2 137.0 %all-gather.18.cloned.1.call-start = ((), (), s32[]{:S(2)}) async-start(), calls=%async_computation.10 | async-start | bytes 3649536 | tf_op jit(solution)/shard_map/all_gather | solution.py:32
  54.5 4.9 copy-start.20
  56.1 3.4 copy-start.18
  57.9 3.1 copy-start.22
  57.9 3.1 copy-start.27
  59.5 44.6 %copy-start.24 = (bf16[384,48]{0,1:T(8,128)(2,1)S(1)}, bf16[384,48]{0,1:T(8,128)(2,1)}, u32[]{:S(2)}) copy-start(bf16[384,48]{0,1:T(8,128)(2,1)} %param.20) | copy-start | bytes 110596
  59.5 88.6 %all-gather.12.cloned.1.call-start = ((), (), s32[]{:S(2)}) async-start(), calls=%async_computation.4 | async-start | bytes 1880064 | tf_op jit(solution)/shard_map/all_gather | solution.py:119
  60.3 204.7 %all-gather.22.cloned.1.call-start = ((), (), s32[]{:S(2)}) async-start(), calls=%async_computation.12 | async-start | bytes 3649536 | tf_op jit(solution)/shard_map/all_gather | solution.py:42
  61.0 207.5 %all-gather.20.cloned.1.call-start = ((), (), s32[]{:S(2)}) async-start(), calls=%async_computation.11 | async-start | bytes 3649536 | tf_op jit(solution)/shard_map/all_gather | solution.py:32
  181.4 2.8 copy-start.8
  184.2 5.9 copy-start.10
  184.2 2.0 copy-start.3
  186.2 1.8 copy-start.7
  188.0 3.8 copy-start
  205.0 8.7 copy-start.28
  211.4 3.6 copy-start.12
  211.4 3.6 collective-permute-start
  221.8 3.2 copy-start.26
  221.8 4.5 copy-start.30
  223.8 74.9 %all-gather.14.cloned.1.call-start = ((), (), s32[]{:S(2)}) async-start(), calls=%async_computation.5 | async-start | bytes 2506752 | tf_op jit(solution)/shard_map/all_gather | solution.py:137
  224.4 138.1 %all-gather.16.cloned.1.call-start = ((), (), s32[]{:S(2)}) async-start(), calls=%async_computation.6 | async-start | bytes 2506752 | tf_op jit(solution)/shard_map/all_gather | solution.py:139
  225.0 194.6 %all-gather.24.cloned.1.call-start = ((), (), s32[]{:S(2)}) async-start(), calls=%async_computation.13 | async-start | bytes 3649536 | tf_op jit(solution)/shard_map/all_gather | solution.py:42
  362.5 15.5 %copy-start.29 = (bf16[768,1536]{1,0:T(8,128)(2,1)S(1)}, bf16[768,1536]{1,0:T(8,128)(2,1)}, u32[]{:S(2)}) copy-start(bf16[768,1536]{1,0:T(8,128)(2,1)} %all-gather.14.cloned.1.call-done) | copy-start | bytes 7077892
  375.8 2.3 copy-start.31
  391.0 3.1 collective-permute-start.2
  401.2 3.4 copy-start.9
  401.2 3.5 copy-start.13
  406.9 1.4 copy-start.5
  409.5 143.7 %reduce-scatter.22.cloned.1.call-start = ((), (), s32[]{:S(2)}) async-start(), calls=%async_computation.14 | async-start | bytes 835584
  410.7 322.4 %all-reduce.28.cloned.1.call-start = ((), (), s32[]{:S(2)}) async-start(), calls=%async_computation.15 | async-start | bytes 9437184
  436.8 7.7 copy-start.6
  436.8 7.7 copy-start.11
  464.4 5.9 copy-start.2
  464.4 5.9 copy-start.4
  502.6 1.7 copy-start.15
  502.6 2.0 copy-start.14
  504.3 2.5 copy-start.16
  504.9 1.9 copy-start.17
  518.5 343.1 %reduce-scatter.16.cloned.1.call-start = ((), (), s32[]{:S(2)}) async-start(), calls=%async_computation.7 | async-start | bytes 1253376 | tf_op jit(solution)/shard_map/reduce_scatter | solution.py:192
  523.3 481.1 %reduce-scatter.18.cloned.1.call-start = ((), (), s32[]{:S(2)}) async-start(), calls=%async_computation.8 | async-start | bytes 5013504 | tf_op jit(solution)/shard_map/reduce_scatter | solution.py:193
  533.2 613.1 %reduce-scatter.20.cloned.1.call-start = ((), (), s32[]{:S(2)}) async-start(), calls=%async_computation.9 | async-start | bytes 5013504 | tf_op jit(solution)/shard_map/reduce_scatter | solution.py:195
  543.2 1.3 copy-start.25
  572.0 56.3 %copy-start.19 = (f32[788]{0:T(1024)S(1)}, f32[788]{0:T(1024)}, u32[]{:S(2)}) copy-start(f32[788]{0:T(1024)} %copy-done.18) | copy-start | bytes 9460
  572.0 56.3 %copy-start.21 = (f32[768]{0:T(1024)S(1)}, f32[768]{0:T(1024)}, u32[]{:S(2)}) copy-start(f32[768]{0:T(1024)} %copy-done.20) | copy-start | bytes 9220
  572.0 56.3 %copy-start.23 = (f32[788]{0:T(1024)S(1)}, f32[788]{0:T(1024)}, u32[]{:S(2)}) copy-start(f32[788]{0:T(1024)} %copy-done.22) | copy-start | bytes 9460
  573.5 47.6 %collective-permute-start.3 = (bf16[4,768]{1,0:T(4,128)(2,1)S(1)}, bf16[4,768]{1,0:T(4,128)(2,1)S(1)}, u32[]{:S(2)}, u32[]{:S(2)}) collective-permute-start(bf16[4,768]{1,0:T(4,128)(2,1)S(1)} %slice.29), channel_id=1, source_target_pairs={{0,1},{2,3},{4,5},{6,7},{8,9},{10,11},{12,13},{14,15},{16,17},{18,... | collective-permute-start | bytes 18440
  575.5 96.6 %collective-permute-start.1 = (bf16[4,768]{1,0:T(4,128)(2,1)S(1)}, bf16[4,768]{1,0:T(4,128)(2,1)S(1)}, u32[]{:S(2)}, u32[]{:S(2)}) collective-permute-start(bf16[4,768]{1,0:T(4,128)(2,1)S(1)} %slice.27), channel_id=1, source_target_pairs={{0,1},{2,3},{4,5},{6,7},{8,9},{10,11},{12,13},{14,15},{16,17},{18,... | collective-permute-start | bytes 18440
Sparse Core Ops, SparseCore 0:
  59.6 11.2 all-gather.17
  73.7 62.8 all-gather.11
  138.1 10.4 all-gather.21
  223.9 8.5 all-gather.19
  235.1 63.5 all-gather.13
  301.3 61.0 all-gather.15
  409.6 9.8 all-gather.23
  424.2 123.5 reduce-scatter.21
  553.6 179.4 all-reduce.27
  739.0 122.5 reduce-scatter.15
  868.2 136.1 reduce-scatter.17
  1010.0 136.2 reduce-scatter.19
where the time goes:
time: 1160 us; the launch traced here: 1150 us
  waiting for transfers between devices  535 us (46%)
  blocking collectives  266 us (23%)
  local copies, waits for them, and re-layouts  152 us (13%)
  matrix products  134 us (12%)
  other arithmetic  40.9 us (4%)
  between operations  17.6 us (2%)
    unnamed x7, blocking collectives  185 us
    reduce_scatter x1, waiting for transfers between devices, local(): lax.psum_scatter(grad_up, 'dp', scatter_dimension=0, tiled=True)  143 us
    reduce_scatter x1, waiting for transfers between devices, local(): lax.psum_scatter(grad_down, 'dp', scatter_dimension=1, tiled=True)  142 us
    reduce_scatter x1, waiting for transfers between devices, local(): lax.psum_scatter(grad_out, 'dp', scatter_dimension=1, tiled=True)  127 us
    unnamed x106, local copies, waits for them, and re-layouts  69.4 us
    unnamed x18, waiting for transfers between devices  51.8 us
    all_gather x1, blocking collectives, local(): lax.all_gather(qv_bias, 'dp', axis=2, tiled=True)  41 us
    all_gather x1, blocking collectives, local(): lax.all_gather(out_weight, 'dp', axis=1, tiled=True)  40.2 us
  transfers between devices with their start and end apart: 16, of which 8 were waited for; matrix products, arithmetic and copies ran while one was open for 25% of the time, Pallas kernels for 0%

commit v1 on v0

--- a/solution.py
+++ b/solution.py
@@ -1,20 +1,807 @@
+import functools
 from functools import partial
-
 import jax
 import jax.numpy as jnp
 from jax import lax
+from jax.experimental import pallas as pl
+from jax.experimental.pallas import tpu as pltpu
 from jax.sharding import PartitionSpec as P
 
+MESH = pl.DeviceIdType.MESH
+BF = jnp.bfloat16
+F32 = jnp.float32
+DMA = pltpu.SemaphoreType.DMA
 HD = 64
 SEQ = 197
-
-
-epsilon = 1e-06
+SP = 208
+QUAD = 256
+EPS = 1e-06
+X = Y = 2
+ALL = slice(None)
+
+
+def dot(a, b, ca=1, cb=0):
+    return lax.dot_general(a, b, (((ca,), (cb,)), ((), ())), preferred_element_type=F32)
+
+
+def remote(src, dst, send, recv, dev):
+    return pltpu.make_async_remote_copy(
+        src_ref=src, dst_ref=dst, send_sem=send, recv_sem=recv, device_id=dev, device_id_type=MESH
+    )
+
+
+def by_core(c, make, op):
+    for core in range(2):
+
+        @pl.when(c == core)
+        def _(core=core):
+            getattr(make(core), op)()
+
+
+def center(x):
+    d = x - jnp.mean(x, axis=-1, keepdims=True)
+    r = lax.rsqrt(jnp.mean(d * d, axis=-1, keepdims=True) + EPS)
+    return d * r, r
+
+
+class Place:
+    def __init__(self, zs):
+        dp = lax.axis_index("dp")
+        self.c = lax.axis_index("tensor")
+        self.zs = zs
+        self.z = dp // (X * Y)
+        self.y = (dp // X) % Y
+        self.x = dp % X
+        self.dp = dp
+
+    def dev(self, z, y, x, c):
+        return {"dp": (z * Y + y) * X + x, "tensor": c}
+
+    def zdev(self, k):
+        return self.dev(lax.rem(self.z + k, self.zs), self.y, self.x, self.c)
+
+    def xdev(self):
+        return self.dev(self.z, self.y, 1 - self.x, self.c)
+
+    def ydev(self):
+        return self.dev(self.z, 1 - self.y, self.x, self.c)
+
+    def cdev(self):
+        return self.dev(self.z, self.y, self.x, 1 - self.c)
+
+    def greet(self):
+        barrier = pltpu.get_barrier_semaphore()
+        peers = [self.xdev(), self.ydev(), self.cdev()] + [self.zdev(k) for k in range(1, self.zs)]
+        for peer in peers:
+            pl.semaphore_signal(barrier, inc=1, device_id=peer, device_id_type=MESH)
+        pl.semaphore_wait(barrier, len(peers))
+
+
+PIECES = (
+    ("s", 0, 0, 128),
+    ("a", 0, 0, 384),
+    ("a", 1, 0, 384),
+    ("a", 2, 0, 384),
+    ("a", 3, 0, 384),
+    ("b", 0, 0, 768),
+    ("b", 0, 768, 768),
+    ("b", 1, 0, 768),
+    ("b", 1, 768, 768),
+)
+NP = len(PIECES)
+HALF = {"a": 384, "b": 1536}
+
+
+class Gather:
+    def __init__(self, place, shards, fulls, sems):
+        self.place, self.shards, self.fulls = place, shards, fulls
+        self.zs, self.zr, self.fs, self.fr, self.gs, self.gr, self.ps, self.pr, self.ls = sems
+
+    def full(self, p, idx):
+        name, m, col, width = PIECES[p]
+        ref = self.fulls[name]
+        c = self.place.c
+        if name == "s":
+            return ref.at[(c,) + idx]
+        cols = pl.ds(pl.multiple_of(c * HALF[name] + col, 128), width)
+        return ref.at[(m,) + idx + (ALL, cols)]
+
+    def own(self, p):
+        name, m, col, width = PIECES[p]
+        if name == "s":
+            return self.shards[name]
+        return self.shards[name].at[m, :, pl.ds(col, width)]
+
+    def zcopy(self, p, k):
+        pp = self.place
+        return remote(
+            self.own(p), self.full(p, (pp.z, pp.y, pp.x)), self.zs.at[p, k - 1], self.zr.at[p, k - 1], pp.zdev(k)
+        )
+
+    def local(self, p):
+        pp = self.place
+        return pltpu.make_async_copy(self.own(p), self.full(p, (pp.z, pp.y, pp.x)), self.ls.at[p])
+
+    def first(self, p, core):
+        pp = self.place
+        s = self.full(p, (ALL, pp.y, pp.x))
+        return remote(s, s, self.fs.at[p], self.fr.at[p], pp.xdev() if core == 0 else pp.ydev())
+
+    def second(self, p, core):
+        pp = self.place
+        s = self.full(p, (ALL, pp.y, ALL) if core == 0 else (ALL, ALL, pp.x))
+        return remote(s, s, self.gs.at[p], self.gr.at[p], pp.ydev() if core == 0 else pp.xdev())
+
+    def pair(self, p):
+        s = self.full(p, (ALL, ALL, ALL))
+        return remote(s, s, self.ps.at[p], self.pr.at[p], self.place.cdev())
+
+    def start_z(self, p):
+        self.local(p).start()
+        for k in range(1, self.place.zs):
+            self.zcopy(p, k).start()
+
+    def tick(self, t, ahead=2):
+        c = self.place.c
+        if t < NP:
+            self.local(t).wait()
+            for k in range(1, self.place.zs):
+                self.zcopy(t, k).wait_recv()
+            if t + ahead < NP:
+                self.start_z(t + ahead)
+            by_core(c, functools.partial(self.first, t), "start")
+        if 0 <= t - 1 < NP:
+            by_core(c, functools.partial(self.first, t - 1), "wait_recv")
+            by_core(c, functools.partial(self.second, t - 1), "start")
+        if 0 <= t - 2 < NP:
+            by_core(c, functools.partial(self.second, t - 2), "wait_recv")
+            self.pair(t - 2).start()
+        if 0 <= t - 3 < NP:
+            self.pair(t - 3).wait_recv()
+
+    def finish(self):
+        c = self.place.c
+        for p in range(NP):
+            for k in range(1, self.place.zs):
+                self.zcopy(p, k).wait_send()
+            by_core(c, functools.partial(self.first, p), "wait_send")
+            by_core(c, functools.partial(self.second, p), "wait_send")
+            self.pair(p).wait_send()
+
+
+def forward_kernel(zs, images, *refs):
+    (a_sh, b_sh, s_sh, tok) = refs[:4]
+    outs = refs[4:17]
+    (wa_o, wb_o, h1_o, qkv_o, p_o, att_o, mid_o, h2_o, hid_o, gp_o, lo_o, vec_o, upb_o) = outs
+    (wa, wb, sv, h1, qkv, pbuf, att, mid, h2, hid, gp, lo, acc, psem, osem) = refs[17:32]
+    sems = refs[32:]
+    rows = images * SP
+    place = Place(zs)
+    n = zs * Y * X
+    place.greet()
+    g = Gather(place, {"a": a_sh, "b": b_sh, "s": s_sh}, {"a": wa, "b": wb, "s": sv}, sems)
+    for p in range(2):
+        g.start_z(p)
+    for t in range(4):
+        g.tick(t)
+
+    cell = 768 // (2 * n)
+    flat = sv[...].reshape(2 * n * 16, 128)
+    lane = lax.broadcasted_iota(jnp.int32, (128, 768), 0)
+    col = lax.broadcasted_iota(jnp.int32, (128, 768), 1)
+    spread = dot(flat, (lax.rem(col, cell) == lane).astype(BF)).reshape(2 * n, 16, 768)
+    who = lax.broadcasted_iota(jnp.int32, (2 * n, 16, 768), 0)
+    kind = lax.broadcasted_iota(jnp.int32, (2 * n, 16, 768), 1)
+    spot = lax.broadcasted_iota(jnp.int32, (2 * n, 16, 768), 2) // cell
+    r_of, c_of = lax.rem(who, n), who // n
+    mine = jnp.where(kind < 6, 2 * r_of + c_of, n * c_of + r_of)
+    vec_o[...] = jnp.sum(jnp.where(mine == spot, spread, 0.0), axis=0)
+    cell_up = 1536 // n
+    pick_r = lax.broadcasted_iota(jnp.int32, (2 * n, 2 * n * 16), 0)
+    pick_c = lax.broadcasted_iota(jnp.int32, (2 * n, 2 * n * 16), 1)
+    up_rows = dot((pick_c == pick_r * 16 + 8).astype(BF), flat).astype(BF)
+    lane = lax.broadcasted_iota(jnp.int32, (128, 3072), 0)
+    col = lax.broadcasted_iota(jnp.int32, (128, 3072), 1)
+    spread = dot(up_rows, (lax.rem(col, cell_up) == lane).astype(BF))
+    who = lax.broadcasted_iota(jnp.int32, (2 * n, 3072), 0)
+    spot = lax.broadcasted_iota(jnp.int32, (2 * n, 3072), 1) // cell_up
+    upb_o[...] = jnp.sum(jnp.where(who == spot, spread, 0.0), axis=0, keepdims=True)
+
+    def rows_of(i):
+        return pl.ds(pl.multiple_of(i * SP, 16), SP)
+
+    @pl.loop(0, images)
+    def _(i):
+        v, _r = center(tok[rows_of(i), :].astype(F32))
+        h1[rows_of(i), :] = (v * vec_o[0:1, :] + vec_o[1:2, :]).astype(BF)
+
+    def save(src, dst, k):
+        pltpu.make_async_copy(src, dst, osem.at[k]).start()
+
+    save(h1, h1_o, 0)
+
+    def project(t):
+        @pl.loop(0, 3)
+        def _(j):
+            cols = pl.ds(pl.multiple_of(j * 256, 256), 256)
+            w = wa[t, :, :, :, :, cols].reshape(768, 256)
+            r = dot(h1[...], w)
+            if t == 0:
+                r = (r + vec_o[6:7, cols]).astype(BF) * jnp.asarray(HD**-0.5, BF)
+            elif t == 2:
+                r = r + vec_o[7:8, cols]
+            qkv[t, :, cols] = r.astype(BF)
+
+    for t in range(3):
+        g.tick(4 + t)
+        project(t)
+    save(qkv, qkv_o, 1)
+
+    def attention(i):
+        @pl.loop(0, 3)
+        def _(j):
+            cols = pl.ds(pl.multiple_of(j * QUAD, QUAD), QUAD)
+            step = i * 3 + j
+            slot = lax.rem(step, 2)
+            head = lax.broadcasted_iota(jnp.int32, (SP, QUAD), 1) // HD
+            q = qkv[0, rows_of(i), cols]
+            zero = jnp.zeros_like(q)
+            q4 = jnp.concatenate([jnp.where(head == h, q, zero) for h in range(4)], axis=0)
+            s = dot(q4, qkv[1, rows_of(i), cols], 1, 1)
+            key = lax.broadcasted_iota(jnp.int32, (4 * SP, SP), 1)
+            s = jnp.where(key < SEQ, s, -1e30)
+            e = jnp.exp(s - jnp.max(s, axis=-1, keepdims=True))
+            p = (e * (1.0 / jnp.sum(e, axis=-1, keepdims=True))).astype(BF)
+
+            @pl.when(step >= 2)
+            def _():
+                pltpu.make_async_copy(pbuf.at[slot], p_o.at[step - 2], psem.at[slot]).wait()
+
+            pbuf[slot] = p
+            pltpu.make_async_copy(pbuf.at[slot], p_o.at[step], psem.at[slot]).start()
+            o4 = dot(p, qkv[2, rows_of(i), cols])
+            o = jnp.zeros((SP, QUAD), F32)
+            for h in range(4):
+                o = jnp.where(head == h, o4[h * SP : (h + 1) * SP], o)
+            att[rows_of(i), cols] = o.astype(BF)
+
+    done = 7
+    for i in range(images):
+        attention(i)
+        if i % 2 == 1 and done < 8:
+            g.tick(done)
+            done += 1
+    while done < 8:
+        g.tick(done)
+        done += 1
+    steps = images * 3
+    for k in (steps - 2, steps - 1):
+        pltpu.make_async_copy(pbuf.at[k % 2], p_o.at[k], psem.at[k % 2]).wait()
+    save(att, att_o, 2)
+    save(wa, wa_o, 3)
+
+    for j in range(3):
+        w = wa[3].reshape(768, 768)[j * 256 : (j + 1) * 256, :]
+        cols = slice(j * 256, (j + 1) * 256)
+        mid[:, cols] = tok[:, cols].astype(F32) + (dot(att[...], w, 1, 1) + vec_o[2:3, cols])
+
+    @pl.loop(0, images)
+    def _(i):
+        v, _r = center(mid[rows_of(i), :])
+        h2[rows_of(i), :] = (v * vec_o[3:4, :] + vec_o[4:5, :]).astype(BF)
+
+    save(mid, mid_o, 4)
+    save(h2, h2_o, 5)
+
+    def expand(col0):
+        @pl.loop(0, 6)
+        def _(j):
+            start = (j // 3) * 1536 + col0 + (j % 3) * 256
+            cols = pl.ds(pl.multiple_of(start, 256), 256)
+            w = wb[0, :, :, :, :, cols].reshape(768, 256)
+
+            @pl.loop(0, images)
+            def _(i):
+                pre = dot(h2[rows_of(i), :], w) + upb_o[:, cols]
+                cdf = 0.5 + 0.5 * lax.erf(pre * (0.5**0.5))
+                pdf = jnp.exp(pre * pre * -0.5) * 0.3989422804014327
+                hid[rows_of(i), cols] = (pre * cdf).astype(BF)
+                gp[rows_of(i), cols] = (cdf + pre * pdf).astype(BF)
+
+    g.tick(8)
+    expand(0)
+    g.tick(9)
+    expand(768)
+    save(hid, hid_o, 6)
+    save(gp, gp_o, 7)
+
+    def contract(col0, last):
+        for j in range(3):
+            cols = slice(j * 256, (j + 1) * 256)
+            total = mid[:, cols] + vec_o[5:6, cols] if col0 == 0 else acc[:, cols]
+            for half in range(2):
+                fc = slice(half * 1536 + col0, half * 1536 + col0 + 768)
+                w = wb[1, :, :, :, :, fc].reshape(768, 768)[j * 256 : (j + 1) * 256, :]
+                total = total + dot(hid[:, fc], w, 1, 1)
+            if last:
+                lo[:, cols] = total.astype(BF)
+            else:
+                acc[:, cols] = total
+
+    g.tick(10)
+    contract(0, False)
+    g.tick(11)
+    save(wb, wb_o, 8)
+    contract(768, True)
+    save(lo, lo_o, 9)
+    g.finish()
+    pairs = (
+        (h1, h1_o), (qkv, qkv_o), (att, att_o), (wa, wa_o), (mid, mid_o),
+        (h2, h2_o), (hid, hid_o), (gp, gp_o), (wb, wb_o), (lo, lo_o),
+    )
+    for k, (src, dst) in enumerate(pairs):
+        pltpu.make_async_copy(src, dst, osem.at[k]).wait()
+
+
+def forward(a_sh, b_sh, s_sh, tok, zs, images):
+    rows = images * SP
+    n = zs * Y * X
+    S = jax.ShapeDtypeStruct
+    V = pltpu.VMEM
+    outs = (
+        S((4, zs, Y, X, 48, 768), BF), S((2, zs, Y, X, 48, 3072), BF), S((rows, 768), BF), S((3, rows, 768), BF),
+        S((images * 3, 4 * SP, SP), BF), S((rows, 768), BF), S((rows, 768), F32), S((rows, 768), BF),
+        S((rows, 3072), BF), S((rows, 3072), BF), S((rows, 768), BF), S((16, 768), F32), S((1, 3072), F32),
+    )
+    anys = pl.BlockSpec(memory_space=pl.ANY)
+    vm = pl.BlockSpec(memory_space=pltpu.VMEM)
+    return pl.pallas_call(
+        functools.partial(forward_kernel, zs, images),
+        out_shape=outs,
+        in_specs=[vm] * 4,
+        out_specs=[anys] * 11 + [vm] * 2,
+        scratch_shapes=[
+            V((4, zs, Y, X, 48, 768), BF), V((2, zs, Y, X, 48, 3072), BF), V((2, zs, Y, X, 16, 128), BF),
+            V((rows, 768), BF), V((3, rows, 768), BF), V((2, 4 * SP, SP), BF), V((rows, 768), BF), V((rows, 768), F32),
+            V((rows, 768), BF), V((rows, 3072), BF), V((rows, 3072), BF), V((rows, 768), BF), V((rows, 768), F32),
+            DMA((2,)), DMA((10,)),
+            DMA((NP, zs - 1)), DMA((NP, zs - 1)), DMA((NP,)), DMA((NP,)), DMA((NP,)), DMA((NP,)), DMA((NP,)), DMA((NP,)), DMA((NP,)),
+        ],
+        compiler_params=pltpu.CompilerParams(collective_id=1, has_side_effects=True, vmem_limit_bytes=60 * 2**20),
+        name="gather_forward",
+    )(a_sh, b_sh, s_sh, tok)
+
+
+def pack_small(n1g, n1s, ob, n2g, n2s, db, qv, upb):
+    cells = [n1g, n1s, ob, n2g, n2s, db, qv[0, 0], qv[1, 0]]
+    parts = [jnp.pad(v, (0, 128 - v.shape[0])) for v in cells] + [jnp.pad(upb[0], (0, 128 - upb.shape[1]))]
+    return jnp.pad(jnp.stack(parts), ((0, 7), (0, 0)))
+
+
+def pad_rows(v, images):
+    return jnp.pad(v.reshape(images, SEQ, v.shape[1]), ((0, 0), (0, SP - SEQ), (0, 0))).reshape(images * SP, v.shape[1])
+
+
+PLAN = {
+    "dn10": [(0, 1)],
+    "pre0": [(1, 1)],
+    "pre2": [(0, 2)],
+    "up00": [(0, 3)],
+    "up01": [(2, 1)],
+    "up11": [(3, 1)],
+    "dh20": [(1, 2)],
+    "dh21": [(0, 4)],
+    "dh22": [(1, 3)],
+    "out": [(2, 2), (1, 4)],
+    "datt": [(4, 1), (2, 3)],
+    "attn0": [(3, 2), (2, 4)],
+    "attn1": [(3, 3), (4, 2)],
+    "attn2": [(3, 4), (4, 3)],
+    "attn3": [(4, 4)],
+    "qkv1": [(5, 1)],
+    "qkv2": [(6, 1)],
+    "dh10": [(7, 1), (5, 2)],
+    "dh11": [(6, 2), (5, 3)],
+    "dh12": [(7, 2), (5, 4), (6, 3)],
+    "small": [(8, 1), (6, 4), (7, 3), (8, 2), (7, 4), (8, 3), (8, 4)],
+}
+
+
+SPIECES = (
+    ("b", 1, 0, 768),
+    ("b", 1, 768, 768),
+    ("b", 0, 0, 768),
+    ("b", 0, 768, 768),
+    ("a", 3, 0, 384),
+    ("a", 0, 0, 384),
+    ("a", 1, 0, 384),
+    ("a", 2, 0, 384),
+    ("s", 0, 0, 128),
+)
+NS = len(SPIECES)
+
+
+class Scatter:
+    def __init__(self, place, gdn, gout, gs, wb, pb, pa, psm, rb, ra, rs, outs, sems):
+        self.place = place
+        self.gdn, self.gout, self.gs_, self.wb = gdn, gout, gs, wb
+        self.pbuf = {"b": pb, "a": pa, "s": psm}
+        self.rbuf = {"b": rb, "a": ra, "s": rs}
+        self.outs = outs
+        self.s_send, self.s_recv, self.z_send, self.z_recv = sems
+
+    def index(self, p):
+        return p if p < 4 else (p - 4 if p < 8 else 0)
+
+    def part(self, p, own):
+        if p < 2:
+            return self.gdn.at[p, own]
+        if p < 4:
+            cols = pl.ds(pl.multiple_of((p - 2) * 1536 + own * 768, 128), 768)
+            return self.wb.at[1, :, :, :, :, cols]
+        if p == 4:
+            return self.gout.at[own]
+        if p < 8:
+            k = p - 5
+            return self.gdn.at[k // 2, own, :, :, :, :, pl.ds((k % 2) * 384, 384)]
+        return self.gs_.at[own]
+
+    def precv(self, p):
+        return self.pbuf[SPIECES[p][0]].at[self.index(p)]
+
+    def recv(self, p, k):
+        return self.rbuf[SPIECES[p][0]][k].at[self.index(p)]
+
+    def pair(self, p):
+        return remote(self.part(p, 0), self.precv(p), self.s_send.at[p, 0], self.s_recv.at[p, 0], self.place.cdev())
+
+    def one(self, p, core):
+        pp, s = self.place, self.part(p, 1)
+        src = s.at[:, 1 - pp.y, :] if core == 0 else s.at[:, :, 1 - pp.x]
+        return remote(src, self.recv(p, 0), self.s_send.at[p, 1], self.s_recv.at[p, 1], pp.ydev() if core == 0 else pp.xdev())
+
+    def two(self, p, core):
+        pp, s = self.place, self.part(p, 1)
+        src = s.at[:, pp.y, 1 - pp.x] if core == 0 else s.at[:, 1 - pp.y, pp.x]
+        return remote(src, self.recv(p, 1), self.s_send.at[p, 2], self.s_recv.at[p, 2], pp.xdev() if core == 0 else pp.ydev())
+
+    def three(self, p, k):
+        pp, s = self.place, self.part(p, 1)
+        to = lax.rem(pp.z + k, pp.zs)
+        return remote(
+            s.at[to, pp.y, pp.x], self.recv(p, 2).at[k - 1], self.z_send.at[p, k - 1], self.z_recv.at[p, k - 1], pp.zdev(k)
+        )
+
+    def stage(self, p, k):
+        pp = self.place
+        c = pp.c
+        zs = pp.zs
+        kind = F32 if p == 8 else BF
+        s = self.part(p, 1)
+        if k == 0:
+            self.pair(p).start()
+        elif k == 1:
+            self.pair(p).wait_recv()
+            r = self.precv(p)
+            for zz in range(zs):
+                s[zz] = (s[zz].astype(F32) + r[zz].astype(F32)).astype(kind)
+            by_core(c, functools.partial(self.one, p), "start")
+        elif k == 2:
+            by_core(c, functools.partial(self.one, p), "wait_recv")
+            r = self.recv(p, 0)
+            for zz in range(zs):
+                for j in range(2):
+                    yi, xi = jnp.where(c == 0, pp.y, j), jnp.where(c == 0, j, pp.x)
+                    s[zz, yi, xi] = (s[zz, yi, xi].astype(F32) + r[zz, j].astype(F32)).astype(kind)
+            by_core(c, functools.partial(self.two, p), "start")
+        elif k == 3:
+            by_core(c, functools.partial(self.two, p), "wait_recv")
+            r = self.recv(p, 1)
+            for zz in range(zs):
+                s[zz, pp.y, pp.x] = (s[zz, pp.y, pp.x].astype(F32) + r[zz].astype(F32)).astype(kind)
+            for k in range(1, zs):
+                self.three(p, k).start()
+        else:
+            r = self.recv(p, 2)
+            total = s[pp.z, pp.y, pp.x].astype(F32)
+            for k in range(1, zs):
+                self.three(p, k).wait_recv()
+                total = total + r[k - 1].astype(F32)
+            name, m, col, width = SPIECES[p]
+            if name == "s":
+                self.outs[name][...] = total
+            else:
+                self.outs[name][m, :, pl.ds(col, width)] = total
+            self.pair(p).wait_send()
+            by_core(c, functools.partial(self.one, p), "wait_send")
+            by_core(c, functools.partial(self.two, p), "wait_send")
+            for k in range(1, zs):
+                self.three(p, k).wait_send()
+
+
+def backward_kernel(zs, images, plan, *refs):
+    (wa_i, wb_i, h1_i, qkv_i, p_i, att_i, mid_i, h2_i, hid_i, gp_i, tok_i, cot_i, vec) = refs[:13]
+    dx_o, ga_o, gb_o, gs_o = refs[13:17]
+    (wa, wb, cot, h2, qkv, att, mid, dh, dpre, db, hidt, pt, xt, yt, vg, ug, gdn, gout, gs) = refs[17:36]
+    pb, pa, psm = refs[36:39]
+    rb, ra, rs = refs[39:42], refs[42:45], refs[45:48]
+    lsem, hsem, psem = refs[48:51]
+    sems = refs[51:]
+    n = zs * Y * X
+    rows = images * SP
+    place = Place(zs)
+    c = place.c
+    sc = Scatter(place, gdn, gout, gs, wb, pb, pa, psm, rb, ra, rs, {"a": ga_o, "b": gb_o, "s": gs_o}, sems)
+
+    loads = {
+        "cot": (cot_i, cot), "dn": (wb_i.at[1], wb.at[1]), "gp": (gp_i, dpre), "h2": (h2_i, h2), "up": (wb_i.at[0], wb.at[0]),
+        "mid": (mid_i, mid), "att": (att_i, att), "wa": (wa_i, wa), "qkv": (qkv_i, qkv), "h1": (h1_i, cot), "tok": (tok_i, h2),
+    }
+    names = list(loads)
+
+    def load(name):
+        src, dst = loads[name]
+        return pltpu.make_async_copy(src, dst, lsem.at[names.index(name)])
+
+    def hcols(step):
+        own = (step // 3) % 2
+        half = jnp.where(own == 1, c, 1 - c)
+        return pl.ds(pl.multiple_of(half * 1536 + (step // 6) * 768 + (step % 3) * 256, 256), 256)
+
+    def htile(step):
+        slot = step % 3
+        return pltpu.make_async_copy(hid_i.at[:, hcols(step)], hidt.at[slot], hsem.at[slot])
+
+    load("cot").start()
+    for k in range(2):
+        htile(k).start()
+    for name in ("dn", "gp", "h2", "up", "mid", "att", "wa", "qkv"):
+        load(name).start()
+    place.greet()
+
+    def after(key):
+        for p, k in plan.get(key, ()):
+            sc.stage(p, k)
+
+    def rows_of(i):
+        return pl.ds(pl.multiple_of(i * SP, 16), SP)
+
+    def cut(v):
+        return v.reshape(zs, Y, X, 48, v.shape[1])
+
+    vg[...] = jnp.zeros_like(vg)
+    load("cot").wait()
+    xt[...] = cot[...].T
+    vg[5:6, :] = jnp.sum(cot[...].astype(F32), axis=0, keepdims=True)
+
+    for piece in range(2):
+        for own in range(2):
+
+            @pl.loop(0, 3)
+            def _(j, piece=piece, own=own):
+                step = piece * 6 + own * 3 + j
+                htile(step).wait()
+
+                @pl.when(step + 2 < 12)
+                def _():
+                    htile(step + 2).start()
+
+                gdn[piece, own, :, :, :, :, pl.ds(pl.multiple_of(j * 256, 256), 256)] = cut(
+                    dot(xt[...], hidt[step % 3]).astype(BF)
+                )
+
+            if own == 0:
+                sc.stage(piece, 0)
+            after(f"dn{piece}{own}")
+
+    load("dn").wait()
+    load("gp").wait()
+    for part in range(4):
+
+        @pl.loop(0, 3)
+        def _(j, part=part):
+            cols = pl.ds(pl.multiple_of(part * 768 + j * 256, 256), 256)
+            w = wb[1, :, :, :, :, cols].reshape(768, 256)
+            d = (dot(cot[...], w) * dpre[:, cols].astype(F32)).astype(BF)
+            dpre[:, cols] = d
+            ug[:, cols] = jnp.sum(d.astype(F32), axis=0, keepdims=True)
+
+        after(f"pre{part}")
+    load("h2").wait()
+    yt[...] = h2[...].T
+    load("tok").start()
+    for piece in range(2):
+        for own in range(2):
+
+            @pl.loop(0, 3)
+            def _(j, piece=piece, own=own):
+                half = c if own == 1 else 1 - c
+                cols = pl.ds(pl.multiple_of(half * 1536 + piece * 768 + j * 256, 256), 256)
+                dest = pl.ds(pl.multiple_of(piece * 1536 + own * 768 + j * 256, 256), 256)
+                wb[1, :, :, :, :, dest] = cut(dot(yt[...], dpre[:, cols]).astype(BF))
+
+            if own == 0:
+                sc.stage(2 + piece, 0)
+            after(f"up{piece}{own}")
+
+    load("up").wait()
+    for j in range(3):
+        w = wb[0].reshape(768, 3072)[j * 256 : (j + 1) * 256, :]
+        dh[:, j * 256 : (j + 1) * 256] = dot(dpre[...], w, 1, 1)
+        after(f"dh2{j}")
+    load("mid").wait()
+
+    @pl.loop(0, images)
+    def _(i):
+        v, r = center(mid[rows_of(i), :])
+        g = dh[rows_of(i), :]
+        vg[3:4, :] += jnp.sum(g * v, axis=0, keepdims=True)
+        vg[4:5, :] += jnp.sum(g, axis=0, keepdims=True)
+        dn = g * vec[3:4, :]
+        d = cot[rows_of(i), :].astype(F32) + r * (
+            dn - jnp.mean(dn, axis=-1, keepdims=True) - v * jnp.mean(dn * v, axis=-1, keepdims=True)
+        )
+        dh[rows_of(i), :] = d
+        low = d.astype(BF)
+        db[rows_of(i), :] = low
+        vg[2:3, :] += jnp.sum(low.astype(F32), axis=0, keepdims=True)
+
+    load("h1").start()
+    after("norm2")
+    xt[...] = db[...].T
+    load("att").wait()
+    for h in range(2):
+        own = jnp.where(c == h, 1, 0)
+        gout[own] = cut(dot(xt[...], att[:, h * 384 : (h + 1) * 384]).astype(BF))
+    sc.stage(4, 0)
+    after("out")
+    load("wa").wait()
+
+    @pl.loop(0, 3)
+    def _(j):
+        cols = pl.ds(pl.multiple_of(j * 256, 256), 256)
+        att[:, cols] = dot(db[...], wa[3, :, :, :, :, cols].reshape(768, 256)).astype(BF)
+
+    after("datt")
+    load("qkv").wait()
+
+    def ptile(step):
+        return pltpu.make_async_copy(p_i.at[step], pt.at[step % 2], psem.at[step % 2])
+
+    ptile(0).start()
+    total = images * 3
+    for i in range(images):
+
+        @pl.loop(0, 3)
+        def _(j, i=i):
+            cols = pl.ds(pl.multiple_of(j * QUAD, QUAD), QUAD)
+            step = i * 3 + j
+            ptile(step).wait()
+
+            @pl.when(step + 1 < total)
+            def _():
+                ptile(step + 1).start()
+
+            head = lax.broadcasted_iota(jnp.int32, (SP, QUAD), 1) // HD
+            q, k, v, do = qkv[0, rows_of(i), cols], qkv[1, rows_of(i), cols], qkv[2, rows_of(i), cols], att[rows_of(i), cols]
+            zero = jnp.zeros_like(q)
+            q4 = jnp.concatenate([jnp.where(head == h, q, zero) for h in range(4)], axis=0)
+            do4 = jnp.concatenate([jnp.where(head == h, do, zero) for h in range(4)], axis=0)
+            p = pt[step % 2]
+            dp = dot(do4, v, 1, 1)
+            dv = dot(p, do4, 0, 0)
+            pf = p.astype(F32)
+            ds = (pf * (dp - jnp.sum(pf * dp, axis=-1, keepdims=True))).astype(BF)
+            dq4 = dot(ds, k)
+            dk = dot(ds, q4, 0, 0)
+            dq = jnp.zeros((SP, QUAD), F32)
+            for h in range(4):
+                dq = jnp.where(head == h, dq4[h * SP : (h + 1) * SP], dq)
+            qkv[0, rows_of(i), cols] = (dq * HD**-0.5).astype(BF)
+            qkv[1, rows_of(i), cols] = dk.astype(BF)
+            qkv[2, rows_of(i), cols] = dv.astype(BF)
+
+        after(f"attn{i}")
+
+    load("h1").wait()
+    yt[...] = cot[...].T
+    vg[6:7, :] = jnp.sum(qkv[0].astype(F32), axis=0, keepdims=True)
+    vg[7:8, :] = jnp.sum(qkv[2].astype(F32), axis=0, keepdims=True)
+    for t in range(3):
+        for h in range(2):
+            own = jnp.where(c == h, 1, 0)
+            gdn[t // 2, own, :, :, :, :, (t % 2) * 384 : (t % 2) * 384 + 384] = cut(
+                dot(yt[...], qkv[t, :, h * 384 : (h + 1) * 384]).astype(BF)
+            )
+        sc.stage(5 + t, 0)
+        after(f"qkv{t}")
+
+    for j in range(3):
+        cols = slice(j * 256, (j + 1) * 256)
+        sum_ = None
+        for t in range(3):
+            w = wa[t].reshape(768, 768)[cols, :]
+            r = dot(qkv[t], w, 1, 1)
+            sum_ = r if sum_ is None else sum_ + r
+        mid[:, cols] = sum_
+        after(f"dh1{j}")
+    load("tok").wait()
+
+    @pl.loop(0, images)
+    def _(i):
+        v, r = center(h2[rows_of(i), :].astype(F32))
+        g = mid[rows_of(i), :]
+        vg[0:1, :] += jnp.sum(g * v, axis=0, keepdims=True)
+        vg[1:2, :] += jnp.sum(g, axis=0, keepdims=True)
+        dn = g * vec[0:1, :]
+        mid[rows_of(i), :] = dh[rows_of(i), :] + r * (
+            dn - jnp.mean(dn, axis=-1, keepdims=True) - v * jnp.mean(dn * v, axis=-1, keepdims=True)
+        )
+
+    done = pltpu.make_async_copy(mid, dx_o, lsem.at[len(names)])
+    done.start()
+
+    def two_parts(v):
+        hi = v.astype(BF)
+        return hi, (v - hi.astype(F32)).astype(BF)
+
+    cell = 768 // (2 * n)
+    who = lax.broadcasted_iota(jnp.int32, (2 * n, 16, 768), 0)
+    kind = lax.broadcasted_iota(jnp.int32, (2 * n, 16, 768), 1)
+    spot = lax.broadcasted_iota(jnp.int32, (2 * n, 16, 768), 2) // cell
+    r_of, c_of = lax.rem(who, n), who // n
+    mine = jnp.where(kind < 6, 2 * r_of + c_of, n * c_of + r_of)
+    mixed = jnp.where(mine == spot, vg[...][None], 0.0).reshape(2 * n * 16, 768)
+    pick = (lax.rem(lax.broadcasted_iota(jnp.int32, (768, 128), 0), cell) == lax.broadcasted_iota(jnp.int32, (768, 128), 1)).astype(BF)
+    small = sum(dot(part, pick) for part in two_parts(mixed)).reshape(2 * n, 16, 128)
+    cell_up = 1536 // n
+    who = lax.broadcasted_iota(jnp.int32, (2 * n, 3072), 0)
+    spot = lax.broadcasted_iota(jnp.int32, (2 * n, 3072), 1) // cell_up
+    mixed = jnp.where(who == spot, ug[...], 0.0)
+    pick = (lax.rem(lax.broadcasted_iota(jnp.int32, (3072, 128), 0), cell_up) == lax.broadcasted_iota(jnp.int32, (3072, 128), 1)).astype(BF)
+    up_part = sum(dot(part, pick) for part in two_parts(mixed)).reshape(2 * n, 1, 128)
+    kind = lax.broadcasted_iota(jnp.int32, (2 * n, 16, 128), 1)
+    small = jnp.where(kind == 8, up_part, small).reshape(2, zs, Y, X, 16, 128)
+    for h in range(2):
+        gs[jnp.where(c == h, 1, 0)] = small[h]
+    sc.stage(8, 0)
+    after("small")
+    done.wait()
+
+
+def backward(saved, tok, cot, vec, zs, images, plan):
+    rows = images * SP
+    S = jax.ShapeDtypeStruct
+    V = pltpu.VMEM
+    dims = (zs, Y, X)
+    anys = pl.BlockSpec(memory_space=pl.ANY)
+    vm = pl.BlockSpec(memory_space=pltpu.VMEM)
+    return pl.pallas_call(
+        functools.partial(backward_kernel, zs, images, plan),
+        out_shape=(S((rows, 768), F32), S((4, 48, 384), F32), S((2, 48, 1536), F32), S((16, 128), F32)),
+        in_specs=[anys] * 12 + [vm],
+        out_specs=[anys] + [vm] * 3,
+        scratch_shapes=[
+            V((4,) + dims + (48, 768), BF), V((2,) + dims + (48, 3072), BF), V((rows, 768), BF), V((rows, 768), BF),
+            V((3, rows, 768), BF), V((rows, 768), BF), V((rows, 768), F32), V((rows, 768), F32), V((rows, 3072), BF),
+            V((rows, 768), BF), V((3, rows, 256), BF), V((2, 4 * SP, SP), BF), V((768, rows), BF), V((768, rows), BF),
+            V((16, 768), F32), V((1, 3072), F32),
+            V((2, 2) + dims + (48, 768), BF), V((2,) + dims + (48, 384), BF), V((2,) + dims + (16, 128), F32),
+            V((4,) + dims + (48, 768), BF), V((4,) + dims + (48, 384), BF), V((1,) + dims + (16, 128), F32),
+            V((4, zs, 2, 48, 768), BF), V((4, zs, 48, 768), BF), V((4, zs - 1, 48, 768), BF),
+            V((4, zs, 2, 48, 384), BF), V((4, zs, 48, 384), BF), V((4, zs - 1, 48, 384), BF),
+            V((1, zs, 2, 16, 128), F32), V((1, zs, 16, 128), F32), V((1, zs - 1, 16, 128), F32),
+            DMA((12,)), DMA((3,)), DMA((2,)),
+            DMA((NS, 3)), DMA((NS, 3)), DMA((NS, zs - 1)), DMA((NS, zs - 1)),
+        ],
+        compiler_params=pltpu.CompilerParams(collective_id=2, has_side_effects=True, vmem_limit_bytes=60 * 2**20),
+        name="backward_scatter",
+    )(*saved, tok, cot, vec)
 
 
 def normalize(values):
     centered = values - jnp.mean(values, axis=-1, keepdims=True)
-    inverse = lax.rsqrt(jnp.mean(centered * centered, axis=-1, keepdims=True) + epsilon)
+    inverse = lax.rsqrt(jnp.mean(centered * centered, axis=-1, keepdims=True) + EPS)
     return (centered * inverse, inverse)
 
 
@@ -222,7 +1009,30 @@
     )
 
 
+def local_fused(zs, tokens, cotangent, norm1_gain, norm1_shift, qkv_weight, qv_bias, out_weight, out_bias,
+                norm2_gain, norm2_shift, up_weight, up_bias, down_weight, down_bias):
+    images = tokens.shape[0] // SEQ
+    a = jnp.concatenate([qkv_weight, out_weight.T[None]], 0)
+    b = jnp.stack([up_weight, down_weight.T])
+    s = pack_small(norm1_gain, norm1_shift, out_bias, norm2_gain, norm2_shift, down_bias, qv_bias, up_bias)
+    tok = pad_rows(tokens, images)
+    o = forward(a, b, s, tok, zs, images)
+    dx, ga, gb, gs = backward(o[:10], tok, pad_rows(cotangent, images), o[11], zs, images, PLAN)
+    cell = norm1_gain.shape[0]
+
+    def unpad(v):
+        return v.reshape(images, SP, -1)[:, :SEQ].reshape(images * SEQ, -1)
+
+    return (
+        unpad(o[10]), unpad(dx), gs[0, :cell], gs[1, :cell], ga[:3], gs[6:8, None, :cell], ga[3].T, gs[2, :cell],
+        gs[3, :cell], gs[4, :cell], gb[0], gs[8:9, : up_bias.shape[1]], gb[1].T, gs[5, :cell],
+    )
+
+
 def solution(mesh):
+    size = mesh.shape["dp"]
+    zs = size // (X * Y)
+    fused = size == zs * X * Y and mesh.shape["tensor"] == 2 and 768 // size == 48
     placed = (
         P(("dp", "tensor"), None),
         P(("dp", "tensor"), None),
@@ -240,7 +1050,7 @@
         P(("dp", "tensor")),
     )
     return jax.shard_map(
-        local,
+        partial(local_fused, zs) if fused else local,
         mesh=mesh,
         in_specs=placed,
         out_specs=(

time: 1160 us -> 250 us (0.22)
  waiting for transfers between devices: 535 us -> 0 us
  blocking collectives: 266 us -> 0 us
  Pallas kernels: 0 us -> 223 us
  matrix products: 134 us -> 0 us
  local copies, waits for them, and re-layouts: 152 us -> 19 us
  other arithmetic: 40.9 us -> 3.32 us
  between operations: 17.6 us -> 0.9 us
    reduce_scatter x3 -> x0, waiting for transfers between devices: 411 us -> none  [the longest x1 143 us: local(): lax.psum_scatter(grad_up, 'dp', scatter_dimension=0, tiled=True)]
    pallas_call x0 -> x2, Pallas kernels: none -> 223 us  [the longest x1 138 us: backward(): pl.pallas_call(functools.partial(backward_kernel, zs, images, plan), out_...]
    unnamed x7 -> x0, blocking collectives: 185 us -> none
    dot_general x18 -> x0, matrix products: 134 us -> none  [the longest x1 27.7 us: local(): jnp.dot(h_two, up_full, preferred_element_type=jnp.float32)]
    all_gather x2 -> x0, blocking collectives: 81.2 us -> none  [the longest x1 41 us: local(): lax.all_gather(qv_bias, 'dp', axis=2, tiled=True)]
    all_gather x7 -> x0, waiting for transfers between devices: 71.5 us -> none  [the longest x1 36.1 us: local(): lax.all_gather(down_weight, 'dp', axis=1, tiled=True)]
    unnamed x106 -> x8, local copies, waits for them, and re-layouts: 69.4 us -> 0.62 us
    unnamed x18 -> x0, waiting for transfers between devices: 51.8 us -> none
  transfers between devices with their start and end apart: 16 -> 0, of which waited for: 8 -> 0; matrix products, arithmetic and copies ran while one was open for 25% -> 0% of each run, Pallas kernels for 0% -> 0%
where the time goes in v1:
time: 250 us; the launch traced here: 246 us
  Pallas kernels  223 us (89%)
  local copies, waits for them, and re-layouts  19 us (8%)
  other arithmetic  3.32 us (1%)
    pallas_call x1, Pallas kernels, backward(): pl.pallas_call(functools.partial(backward_kernel, zs, images, plan), out_...  138 us
    pallas_call x1, Pallas kernels, forward(): pl.pallas_call(functools.partial(forward_kernel, zs, images), out_shape=o...  84.7 us

profile of v1, /device:TPU:0, one launch (start us, length us, event | category | flops | bytes accessed | tf_op | source)
XLA Modules:
  0.0 245.8 jit_solution(11616304045615871184)
XLA Ops:
  0.6 0.7 pad_bitcast_fusion.8
  1.3 0.7 pad_bitcast_fusion.6
  2.0 0.7 slice_bitcast_fusion.9
  2.7 0.7 pad_bitcast_fusion.4
  3.4 0.7 pad_bitcast_fusion
  4.1 0.1 stack.51
  4.1 0.6 pad.49.refs_2_
  4.7 1.6 pad_maximum_fusion.1.refs_0_
  6.3 1.7 pad_maximum_fusion.refs_1_
  8.1 1.6 reshape.52
  9.7 0.0 copy-start
  9.7 1.1 pad.50
  10.8 0.6 copy-done
  11.4 0.3 reshape.56
  11.7 1.1 pad.51
  12.9 84.7 %gather_forward.1 = (bf16[4,4,2,2,48,768]{5,4,3,2,1,0:T(8,128)(2,1)}, bf16[2,4,2,2,48,3072]{5,4,3,2,1,0:T(8,128)(2,1)}, bf16[832,768]{1,0:T(8,128)(2,1)}, bf16[3...) custom-call(bf16[4,48,384]{2,1,0:T(8,128)(2,1)} %pad_maximum_fusion., ...), custom_call_target="tpu_custom_call" | custom-call | tf_op jit(solution)/shard_map/gather_forward/pallas_call | solution.py:358
  97.6 1.4 slice.64
  99.0 1.3 reshape.55
  100.3 137.9 %backward_scatter.1 = (f32[832,768]{1,0:T(8,128)}, f32[4,48,384]{2,1,0:T(8,128)}, f32[2,48,1536]{2,1,0:T(8,128)}, f32[16,128]{1,0:T(8,128)}) custom-call(bf16[4,4,2,2,48,768]{5,4,3,2,1,0:T(8,128)(2,1)} %get-tuple-element.31.refs_0_, bf16[2,4,2,2,48,3072]{5,4,3,2,1,0:T(8,128)(2,1)} %get-tuple-element.32.refs_1_, bf16[832,768]{1,0:T(8,128)(2,1)} %get-tuple-element.33.refs_2_, ...), custom_call_target="tpu_custom_call" | custom-call | tf_op jit(solution)/shard_map/backward_scatter/pallas_call | solution.py:779
  238.2 1.9 slice.65
  240.1 0.0 copy-start.3
  240.1 0.0 copy-start.2
  240.1 0.0 copy-start.1
  240.1 1.7 reshape.59
  241.8 0.0 copy-done.3
  241.8 0.5 slice.61
  242.4 0.6 slice.55
  242.9 0.5 slice_bitcast_fusion.3
  243.5 0.0 copy-done.2
  243.5 0.6 slice_bitcast_fusion.2
  244.1 0.7 slice.54
  244.8 0.0 copy-done.1
  244.8 0.8 slice_bitcast_fusion
  (1 shorter events, 0.0 us)
Async XLA Ops:
  9.7 1.7 copy-start
  240.1 1.7 copy-start.3
  240.1 3.3 %copy-start.2 = (f32[4,48,384]{2,1,0:T(8,128)S(1)}, f32[4,48,384]{2,1,0:T(8,128)}, u32[]{:S(2)}) copy-start(f32[4,48,384]{2,1,0:T(8,128)} %get-tuple-element.44) | copy-start | bytes 884740
  240.1 4.7 %copy-start.1 = (f32[2,48,1536]{2,1,0:T(8,128)S(1)}, f32[2,48,1536]{2,1,0:T(8,128)}, u32[]{:S(2)}) copy-start(f32[2,48,1536]{2,1,0:T(8,128)} %get-tuple-element.45) | copy-start | bytes 1769476
